TPU v7x, 256 devices: a whole 4x4x8 slice. The times are simulated.
256 devices in a mesh: row: 8 (over z_lo, core), col: 8 (over x, z_hi), fsdp: 4 (over y).
Axes of the slice: x: 4, y: 4, z: 8 (z_hi: 2, z_lo: 4; z = z_hi * 4 + z_lo), core: 2. Of those that a mesh axis runs over, the one named last changes fastest.
Arguments:
- video: bfloat16 [4, 3, 64, 256, 256], P('fsdp', None, 'row', 'col'), may hold values from -6 to 6
- kernel: bfloat16 [6912, 256], P(None, 'fsdp'), may hold values from -0.078125 to 0.078125
- bias_vec: float32 [256], replicated, may hold values from -3 to 3
- cotangent: bfloat16 [4, 3, 32, 128, 256], P('fsdp', None, 'row', 'col'), may hold values from -6 to 6
Outputs:
- activated: bfloat16 [4, 3, 32, 128, 256], P('fsdp', None, 'row', 'col')
- video_grad: bfloat16 [4, 3, 64, 256, 256], P('fsdp', None, 'row', 'col')
- kernel_grad: float32 [6912, 256], P(('row', 'col'), 'fsdp')
- bias_grad: float32 [256], replicated
All inputs are finite; a program needn't handle non-finite values.
Results may differ from a plain program's by a relative error of at most 0.007.
Values may be sent and summed in bfloat16 or wider, within the bound.
A program may use at most 64 MiB of HBM per device.

v0:
```python
import math

import jax
import jax.numpy as jnp
from jax import lax
from jax.sharding import PartitionSpec as P


def shifted(shard, axis, by):
    length = lax.axis_size(axis)
    pairs = [(i, i + by) for i in range(length) if 0 <= i + by < length]
    return lax.ppermute(shard, axis, pairs)


def tap_list():
    return [
        (depth_tap, row_tap, col_tap)
        for depth_tap in range(3)
        for row_tap in range(3)
        for col_tap in range(3)
    ]


def gather_taps(padded, height, width):
    frames = padded.shape[0] - 2
    pieces = [
        padded[
            depth_tap : depth_tap + frames,
            row_tap : row_tap + 2 * height - 1 : 2,
            col_tap : col_tap + 2 * width - 1 : 2,
        ]
        for depth_tap, row_tap, col_tap in tap_list()
    ]
    return jnp.concatenate(pieces, axis=3).reshape(frames * height * width, -1)


def spread_taps(columns, frames, height, width, channels):
    parts = columns.reshape(frames, height, width, 27, channels)
    planes = {}
    for number, (depth_tap, row_tap, col_tap) in enumerate(tap_list()):
        row_shift = row_tap // 2
        col_shift = col_tap // 2
        placed = jnp.pad(
            parts[:, :, :, number],
            (
                (depth_tap, 2 - depth_tap),
                (row_shift, 1 - row_shift),
                (col_shift, 1 - col_shift),
                (0, 0),
            ),
        )
        parity = (row_tap % 2, col_tap % 2)
        planes[parity] = placed if parity not in planes else planes[parity] + placed
    upper_pair = jnp.stack([planes[0, 0], planes[0, 1]], axis=3)
    lower_pair = jnp.stack([planes[1, 0], planes[1, 1]], axis=3)
    woven = jnp.stack([upper_pair, lower_pair], axis=2)
    padded = woven.reshape(frames + 2, 2 * height + 2, 2 * width + 2, channels)[
        :, : 2 * height + 1, : 2 * width + 1
    ]
    grid = padded[2:]
    return grid.at[0].add(padded[0] + padded[1])


def times_transpose(rows, weights):
    return lax.dot_general(
        rows, weights, (((1,), (1,)), ((), ())), preferred_element_type=jnp.float32
    )


def body(video, kernel, bias_vec, cotangent):
    frames, tile_rows, tile_cols, channels = video.shape[1:]
    out_rows = tile_rows // 2
    out_cols = tile_cols // 2
    out_channels = cotangent.shape[-1]
    clip = video[0]
    side = shifted(clip[:, :, -1:, :], "col", 1)
    wider = jnp.concatenate([side, clip], axis=2)
    upper = shifted(wider[:, -1:], "row", 1)
    grid = jnp.concatenate([upper, wider], axis=1)
    padded = jnp.concatenate([grid[:1], grid[:1], grid], axis=0)
    patches = gather_taps(padded, out_rows, out_cols)
    preact = (
        jnp.dot(
            patches,
            lax.all_gather(kernel, "fsdp", axis=1, tiled=True),
            preferred_element_type=jnp.float32,
        )
        + bias_vec[None, :]
    )
    sigma = jax.nn.sigmoid(preact)
    activated = (
        (preact * sigma).astype(jnp.bfloat16).reshape(1, frames, out_rows, out_cols, out_channels)
    )
    slope = (
        cotangent[0].reshape(-1, out_channels).astype(jnp.float32)
        * sigma
        * (1.0 + preact * (1.0 - sigma))
    )
    delta = slope.astype(jnp.bfloat16)
    weight_part = lax.dot_general(
        patches, delta, (((0,), (0,)), ((), ())), preferred_element_type=jnp.float32
    )
    bias_part = jnp.sum(delta.astype(jnp.float32), axis=0)
    spread = spread_taps(
        times_transpose(delta, lax.all_gather(kernel, "fsdp", axis=1, tiled=True)),
        frames,
        out_rows,
        out_cols,
        channels,
    )
    returned = shifted(spread[:, :1].astype(jnp.bfloat16), "row", -1).astype(jnp.float32)
    spread = spread[:, 1:]
    spread = spread.at[:, -1:].add(returned)
    returned_side = shifted(spread[:, :, :1], "col", -1)
    spread = spread[:, :, 1:]
    local_grad = spread.at[:, :, -1:].add(returned_side)
    video_grad = local_grad.astype(jnp.bfloat16)[None]
    total_tokens = (
        lax.axis_size("fsdp")
        * frames
        * out_rows
        * out_cols
        * lax.axis_size("row")
        * lax.axis_size("col")
    )
    factor = 1.0 / math.sqrt(total_tokens)
    by_tile = lax.psum_scatter(weight_part, ("row", "col"), scatter_dimension=0, tiled=True)
    summed = lax.psum_scatter(by_tile, "fsdp", scatter_dimension=1, tiled=True)
    kernel_grad = summed * factor
    bias_grad = lax.psum(bias_part, ("row", "col", "fsdp")) * factor
    return (activated, video_grad, kernel_grad, bias_grad)


def solution(mesh):
    return jax.shard_map(
        body,
        mesh=mesh,
        in_specs=(
            P("fsdp", None, "row", "col", None),
            P(None, "fsdp"),
            P(),
            P("fsdp", None, "row", "col", None),
        ),
        out_specs=(
            P("fsdp", None, "row", "col", None),
            P("fsdp", None, "row", "col", None),
            P(("row", "col"), "fsdp"),
            P(),
        ),
        check_vma=False,
    )
```

profile of v0, /device:TPU:2, one launch (start us, length us, event | category | flops | bytes accessed | tf_op | source)
XLA Modules:
  0.0 711.8 jit_solution(3457822603125944996)
XLA Ops:
  8.9 9.1 %collective-permute-start = (bf16[3,8,1,256]{3,2,1,0:T(2,128)(2,1)S(1)}, bf16[3,8,1,256]{3,2,1,0:T(2,128)(2,1)S(1)}, u32[]{:S(2)}, u32[]{:S(2)}) collective-permute-start(bf16[3,8,1,256]{3,2,1,0:T(2,128)(2,1)S(1)} %slice.353), channel_id=1, source_target_pairs={{0,4},{4,8},{8,12},{12,16},{16,20},{20,24},{24,28},{1,5},{5,9},{9,... | collective-permute-start | bytes 36872 | tf_op jit(solution)/shard_map/ppermute | solution.py:12
  18.0 4.7 slice.311
  22.7 4.7 slice.312
  27.4 4.7 slice.314
  32.1 4.7 slice.315
  43.6 3.8 slice.289
  51.0 3.7 slice.291
  62.2 3.7 slice.294
  73.3 3.8 slice.297
  84.5 3.7 slice.300
  95.6 3.7 slice.303
  106.8 3.8 slice.306
  124.7 4.0 convert_reduce_fusion
  129.4 4.0 fusion.11
  133.4 368.9 %fusion = f32[112,256]{1,0:T(8,128)} fusion(f32[6912,256]{1,0:T(8,128)} %fusion.11), kind=kCustom, calls=%all-reduce-scatter | all-reduce-scatter fusion | flops 1835009 | bytes 7193600
  504.4 17.2 %collective-permute-start.5 = (f32[112,256]{1,0:T(8,128)}, f32[112,256]{1,0:T(8,128)}, u32[]{:S(2)}, u32[]{:S(2)}) collective-permute-start(f32[112,256]{1,0:T(8,128)} %fusion), channel_id=1, source_target_pairs={{0,8},{4,12},{8,16},{12,20},{16,24},{20,28},{24,32},{28,36},{32,40... | collective-permute-start | bytes 344072
  522.9 4.1 fusion.10
  527.1 6.9 reshape.128
  533.9 13.1 %fusion.8 = (f32[3,4,16,1,256]{4,3,2,1,0:T(1,128)S(1)}, f32[3,4,16,1,256]{4,3,2,1,0:T(1,128)S(1)}, f32[3,4,16,1,256]{4,3,2,1,0:T(1,128)S(1)}, f32[3,4,16,1,256]{...) fusion(f32[3,4,16,27,256]{4,3,2,1,0:T(8,128)} %reshape.128), kind=kLoop, calls=%fused_computation.85 | loop fusion | bytes 7471104 | tf_op jit(solution)/shard_map/slice | solution.py:44
  547.1 7.0 fusion.9
  554.1 8.9 %collective-permute-start.6 = (f32[28,256]{1,0:T(8,128)S(1)}, f32[28,256]{1,0:T(8,128)S(1)}, u32[]{:S(2)}, u32[]{:S(2)}) collective-permute-start(f32[28,256]{1,0:T(8,128)S(1)} %copy-done.9), channel_id=1, source_target_pairs={{0,12},{4,16},{8,20},{12,24},{16,28},{20,32},{24,36},{28,40},{32,4... | collective-permute-start | bytes 86024
  570.8 104.2 %psum.7 = f32[256]{0:T(256)S(1)} all-reduce(f32[256]{0:T(256)S(1)} %get-tuple-element.56), channel_id=1, replica_groups=mesh['row'=8,'col'=8,'fsdp'=4] {'row','col','fsdp'}, use_global_device_ids=true, to_apply=%region_3.4 | all-reduce | flops 256 | bytes 2048 | tf_op jit(solution)/shard_map/psum | solution.py:130
  675.7 5.3 collective-permute-start.3
  685.5 17.9 %reduce-scatter.6.cloned.1.call-done = f32[64,108]{1,0:T(8,128)} async-done(((f32[256,108]{1,0:T(8,128)}), f32[64,108]{1,0:T(8,128)}) %reduce-scatter.6.cloned.1.call-update) | async-done | bytes 27664
  (127 shorter events, 80.8 us)
Async XLA Ops:
  7.2 35.9 %copy-start = (bf16[1,3,8,32,256]{4,3,2,1,0:T(8,128)(2,1)S(1)}, bf16[1,3,8,32,256]{4,3,2,1,0:T(8,128)(2,1)}, u32[]{:S(2)}) copy-start(bf16[1,3,8,32,256]{4,3,2,1,0:T(8,128)(2,1)} %param.10) | copy-start | bytes 1179652
  7.2 117.5 %all-gather.2.cloned.1.call-start = ((), (), s32[]{:S(2)}) async-start(), calls=%async_computation.1 | async-start | bytes 4423680 | tf_op jit(solution)/shard_map/all_gather | solution.py:85
  7.9 695.5 %reduce-scatter.6.cloned.1.call-start = ((), (), s32[]{:S(2)}) async-start(), calls=%async_computation.2 | async-start | bytes 163840
  8.9 29.8 %collective-permute-start = (bf16[3,8,1,256]{3,2,1,0:T(2,128)(2,1)S(1)}, bf16[3,8,1,256]{3,2,1,0:T(2,128)(2,1)S(1)}, u32[]{:S(2)}, u32[]{:S(2)}) collective-permute-start(bf16[3,8,1,256]{3,2,1,0:T(2,128)(2,1)S(1)} %slice.353), channel_id=1, source_target_pairs={{0,4},{4,8},{8,12},{12,16},{16,20},{20,24},{24,28},{1,5},{5,9},{9,... | collective-permute-start | bytes 36872 | tf_op jit(solution)/shard_map/ppermute | solution.py:12
  39.6 3.5 collective-permute-start.1
  111.7 12.7 %copy-start.8 = (bf16[3,4,16,256]{3,2,1,0:T(8,128)(2,1)S(1)}, bf16[3,4,16,256]{3,2,1,0:T(8,128)(2,1)}, u32[]{:S(2)}) copy-start(bf16[3,4,16,256]{3,2,1,0:T(8,128)(2,1)} %slice.303) | copy-start | bytes 294916
  111.7 12.7 %copy-start.7 = (bf16[3,4,16,256]{3,2,1,0:T(8,128)(2,1)S(1)}, bf16[3,4,16,256]{3,2,1,0:T(8,128)(2,1)}, u32[]{:S(2)}) copy-start(bf16[3,4,16,256]{3,2,1,0:T(8,128)(2,1)} %slice.304) | copy-start | bytes 294916
  111.7 12.8 %copy-start.6 = (bf16[3,4,16,256]{3,2,1,0:T(8,128)(2,1)S(1)}, bf16[3,4,16,256]{3,2,1,0:T(8,128)(2,1)}, u32[]{:S(2)}) copy-start(bf16[3,4,16,256]{3,2,1,0:T(8,128)(2,1)} %slice.305) | copy-start | bytes 294916
  111.7 12.8 %copy-start.5 = (bf16[3,4,16,256]{3,2,1,0:T(8,128)(2,1)S(1)}, bf16[3,4,16,256]{3,2,1,0:T(8,128)(2,1)}, u32[]{:S(2)}) copy-start(bf16[3,4,16,256]{3,2,1,0:T(8,128)(2,1)} %slice.306) | copy-start | bytes 294916
  111.7 13.0 %copy-start.10 = (f32[256]{0:T(256)S(1)}, f32[256]{0:T(256)}, u32[]{:S(2)}) copy-start(f32[256]{0:T(256)} %param.12) | copy-start | bytes 3076
  128.7 0.6 copy-start.3
  133.4 389.5 %copy-start.1 = (bf16[6912,256]{0,1:T(8,128)(2,1)S(1)}, bf16[6912,256]{0,1:T(8,128)(2,1)}, u32[]{:S(2)}) copy-start(bf16[6912,256]{0,1:T(8,128)(2,1)} %all-gather.2.cloned.1.call-done) | copy-start | bytes 10616836
  502.3 178.7 %collective-permute-start.4 = (f32[112,256]{1,0:T(8,128)}, f32[112,256]{1,0:T(8,128)}, u32[]{:S(2)}, u32[]{:S(2)}) collective-permute-start(f32[112,256]{1,0:T(8,128)} %fusion), channel_id=1, source_target_pairs={{0,4},{4,8},{8,12},{12,16},{16,20},{20,24},{24,28},{28,32},{32,36}... | collective-permute-start | bytes 344072
  504.4 176.7 %collective-permute-start.5 = (f32[112,256]{1,0:T(8,128)}, f32[112,256]{1,0:T(8,128)}, u32[]{:S(2)}, u32[]{:S(2)}) collective-permute-start(f32[112,256]{1,0:T(8,128)} %fusion), channel_id=1, source_target_pairs={{0,8},{4,12},{8,16},{12,20},{16,24},{20,28},{24,32},{28,36},{32,40... | collective-permute-start | bytes 344072
  547.1 7.1 copy-start.9
  554.1 126.9 %collective-permute-start.6 = (f32[28,256]{1,0:T(8,128)S(1)}, f32[28,256]{1,0:T(8,128)S(1)}, u32[]{:S(2)}, u32[]{:S(2)}) collective-permute-start(f32[28,256]{1,0:T(8,128)S(1)} %copy-done.9), channel_id=1, source_target_pairs={{0,12},{4,16},{8,20},{12,24},{16,28},{20,32},{24,36},{28,40},{32,4... | collective-permute-start | bytes 86024
  569.4 111.7 %copy-start.2 = (f32[112,256]{1,0:T(8,128)S(1)}, f32[112,256]{1,0:T(8,128)}, u32[]{:S(2)}) copy-start(f32[112,256]{1,0:T(8,128)} %fusion) | copy-start | bytes 344068
  569.5 106.1 %collective-permute-start.2 = (bf16[3,1,33,256]{3,2,1,0:T(8,128)(2,1)S(1)}, bf16[3,1,33,256]{3,2,1,0:T(8,128)(2,1)S(1)}, u32[]{:S(2)}, u32[]{:S(2)}) collective-permute-start(bf16[3,1,33,256]{3,2,1,0:T(8,128)(2,1)S(1)} %slice.413), channel_id=1, source_target_pairs={{32,0},{64,32},{96,64},{128,96},{160,128},{192,160},{224,192},{33,... | collective-permute-start | bytes 152072 | tf_op jit(solution)/shard_map/ppermute | solution.py:12
  675.7 9.6 %collective-permute-start.3 = (f32[3,8,1,256]{3,2,1,0:T(1,128)S(1)}, f32[3,8,1,256]{3,2,1,0:T(1,128)S(1)}, u32[]{:S(2)}, u32[]{:S(2)}) collective-permute-start(f32[3,8,1,256]{3,2,1,0:T(1,128)S(1)} %slice.393), channel_id=1, source_target_pairs={{4,0},{8,4},{12,8},{16,12},{20,16},{24,20},{28,24},{5,1},{9,5},{13... | collective-permute-start | bytes 73736 | tf_op jit(solution)/shard_map/ppermute | solution.py:12
  685.5 19.5 %copy-start.4 = (bf16[3,8,32,256]{3,2,1,0:T(8,128)(2,1)}, bf16[3,8,32,256]{3,2,1,0:T(8,128)(2,1)S(1)}, u32[]{:S(2)}) copy-start(bf16[3,8,32,256]{3,2,1,0:T(8,128)(2,1)S(1)} %scatter-add.14) | copy-start | bytes 1179652
Sparse Core Ops, SparseCore 0:
  9.8 48.3 all-gather.1
  684.1 19.2 reduce-scatter.5
where the time goes:
time: 715 us; the launch traced here: 712 us
  blocking collectives  473 us (66%)
  local copies, waits for them, and re-layouts  142 us (20%)
  starting transfers between devices  45.3 us (6%)
  waiting for transfers between devices  20 us (3%)
  between operations  15.4 us (2%)
  matrix products  12.2 us (2%)
    unnamed x1, blocking collectives  369 us
    psum x1, blocking collectives, body(): bias_grad = lax.psum(bias_part, ('row', 'col', 'fsdp')) * factor  104 us
    slice x27, local copies, waits for them, and re-layouts, gather_taps(): padded[depth_tap:depth_tap + frames, row_tap:row_tap + 2 * height - 1:2,...  87.7 us
    unnamed x4, starting transfers between devices  28.2 us
    unnamed x56, local copies, waits for them, and re-layouts  20.6 us
    slice x2, local copies, waits for them, and re-layouts, spread_taps(): parts[:, :, :, number]  20.2 us
    unnamed x6, waiting for transfers between devices  18.6 us
    ppermute x4, starting transfers between devices, shifted(): return lax.ppermute(shard, axis, pairs)  17.1 us
  transfers between devices with their start and end apart: 9, of which 2 were waited for; matrix products, arithmetic and copies ran while one was open for 21% of the time, Pallas kernels for 0%

commit v1 on v0

v1 whole, which is shorter than its diff:
```python
import math

import jax
import jax.numpy as jnp
from jax import lax
from jax.experimental import pallas as pl
from jax.experimental.pallas import tpu as pltpu
from jax.sharding import PartitionSpec as P

MESH = pl.DeviceIdType.MESH
F32 = jnp.float32
BF16 = jnp.bfloat16

TAPS = 27
CI = 256
CO = 256
SHARD = 64
KROWS = TAPS * CI
TOK = 192
PITCH = 40
VIA_X = 896
ROUND = 4 * VIA_X
DIRECT = KROWS - ROUND
BLOCK = 864
WINDOW = 224
PIECE = 108
FACTOR = 1.0 / math.sqrt(49152)


def frame_of(t, p):
    return max(t + p - 2, 0)


def nt(a, b):
    return lax.dot_general(a, b, (((1,), (1,)), ((), ())), preferred_element_type=F32)


def nn(a, b):
    return jnp.dot(a, b, preferred_element_type=F32)


def identity(n):
    rows = lax.broadcasted_iota(jnp.int32, (n, n), 0)
    cols = lax.broadcasted_iota(jnp.int32, (n, n), 1)
    return (rows == cols).astype(F32).astype(BF16)


PLANE = 27 * PITCH


def take(flat, start, count, stride):
    return jnp.concatenate(
        [flat[pl.ds(n * PLANE + start, count, stride=stride), :] for n in range(2)], axis=1
    )


def put(flat, start, count, stride, value):
    for n in range(2):
        flat[pl.ds(n * PLANE + start, count, stride=stride), :] = value[:, 128 * n : 128 * n + 128]


def swap_halves(value):
    return jnp.concatenate(
        [pltpu.roll(value[:, 128 * n : 128 * n + 128], 64, 1) for n in range(value.shape[1] // 128)],
        axis=1,
    )


def kernel_body(
    video,
    kernel,
    bias,
    cot,
    act_out,
    vg_out,
    kg_out,
    bg_out,
    kin,
    kt,
    vid,
    cotv,
    vpad,
    hl_send,
    hc_send,
    hl,
    hu,
    hc,
    patches,
    pt,
    pts,
    dl,
    dlx,
    dls,
    dlsx,
    w,
    ra,
    rb,
    sa,
    sb,
    ra2,
    rb2,
    tt,
    zz,
    rz,
    by,
    bx,
    bz,
    g,
    gl_send,
    gc_send,
    gu,
    gl,
    gc,
    lsem,
    k_s,
    k_r,
    h_s,
    h_r,
    c_s,
    c_r,
    r1_s,
    r1_r,
    r2_s,
    r2_r,
    r3_s,
    r3_r,
    b_s,
    b_r,
):
    row = lax.axis_index("row")
    col = lax.axis_index("col")
    y = lax.axis_index("fsdp")
    core = lax.rem(row, 2)
    zl = row // 2
    x = col // 2
    zh = lax.rem(col, 2)
    z = zh * 4 + zl

    def to_y(n):
        return {"row": row, "col": col, "fsdp": lax.rem(y + n, 4)}

    def to_x(n):
        return {"row": row, "col": lax.rem(x + n, 4) * 2 + zh, "fsdp": y}

    def to_z(n):
        there = lax.rem(z + n, 8)
        return {
            "row": lax.rem(there, 4) * 2 + core,
            "col": x * 2 + there // 4,
            "fsdp": y,
        }

    def to_tile(rows, cols):
        return {"row": lax.rem(row + rows + 8, 8), "col": lax.rem(col + cols + 8, 8), "fsdp": y}

    sibling = {"row": row + 1 - 2 * core, "col": col, "fsdp": y}

    def remote(src, dst, ss, rs, where):
        return pltpu.make_async_remote_copy(
            src_ref=src, dst_ref=dst, send_sem=ss, recv_sem=rs, device_id=where, device_id_type=MESH
        )

    load_k = pltpu.make_async_copy(kernel, kin, lsem.at[0])
    load_v = pltpu.make_async_copy(video.at[0], vid, lsem.at[1])
    load_c = pltpu.make_async_copy(cot.at[0], cotv, lsem.at[2])
    load_k.start()
    load_v.start()
    load_c.start()

    partners = [to_y(n) for n in (1, 2, 3)] + [to_x(n) for n in (1, 2, 3)]
    partners += [to_z(n) for n in range(1, 8)] + [sibling]
    partners += [to_tile(a, b) for a, b in ((0, 1), (0, -1), (1, 0), (-1, 0), (1, 1), (-1, -1))]
    barrier = pltpu.get_barrier_semaphore()
    for partner in partners:
        pl.semaphore_signal(barrier, inc=1, device_id=partner, device_id_type=MESH)

    own_rows = pl.multiple_of(y * SHARD, SHARD)
    load_k.wait()
    kt[pl.ds(own_rows, SHARD), :] = nt(identity(SHARD), kin[...]).astype(BF16)
    load_v.wait()
    for f in range(3):
        for r in range(8):
            for n in range(2):
                vpad[n, (r + 1) * 3 + f, 8:40, :] = vid[f, r, :, 128 * n : 128 * n + 128].astype(F32)
    flat = vpad.reshape(2 * PLANE, 128)
    hl_send[...] = take(flat, 3 * PITCH + 39, 24, PITCH)
    hc_send[0:3, :] = hl_send[21:24, :]

    pl.semaphore_wait(barrier, len(partners))

    half_rows = pl.multiple_of(y * SHARD + core * 32, 32)
    via = pl.multiple_of(x * VIA_X, 128)

    def shard_rows(n):
        return pl.multiple_of(lax.rem(y + n, 4) * SHARD + core * 32, 32)

    def other_rows(n):
        return pl.multiple_of(lax.rem(y + n, 4) * SHARD + (1 - core) * 32, 32)

    first = []
    for n in (1, 3, 2):
        ref = kt.at[pl.ds(half_rows, 32), pl.ds(via, VIA_X)]
        first.append(remote(ref, ref, k_s.at[n - 1], k_r.at[n - 1], to_y(n)))
        first[-1].start()
    halos = [
        remote(hl_send, hl, h_s.at[0], h_r.at[0], to_tile(0, 1)),
        remote(vid.at[:, 7], hu, h_s.at[1], h_r.at[1], to_tile(1, 0)),
        remote(hc_send, hc, h_s.at[2], h_r.at[2], to_tile(1, 1)),
    ]
    for copy in halos:
        copy.start()
    direct = []
    for n in (1, 3, 2):
        ref = kt.at[pl.ds(half_rows, 32), pl.ds(ROUND, DIRECT)]
        direct.append(remote(ref, ref, k_s.at[2 + n], k_r.at[2 + n], to_y(n)))
        direct[-1].start()

    relayed = []
    for at, n in enumerate((1, 3, 2)):
        first[at].wait_recv()
        rows = shard_rows(4 - n)
        ref = kt.at[pl.ds(rows, 32), pl.ds(via, VIA_X)]
        for m in (1, 3, 2):
            slot = 6 + (n - 1) * 3 + m - 1
            relayed.append(remote(ref, ref, k_s.at[slot], k_r.at[slot], to_x(m)))
            relayed[-1].start()

    for copy in halos:
        copy.wait_recv()
    for f in range(3):
        top = hu[f].astype(F32)
        top = jnp.where(row > 0, top, 0.0)
        for n in range(2):
            vpad[n, f, 8:40, :] = top[:, 128 * n : 128 * n + 128]
    put(flat, 3 * PITCH + 7, 24, PITCH, jnp.where(col > 0, hl[...], 0.0))
    corner = jnp.where((row > 0) & (col > 0), hc[...], 0.0)
    for f in range(3):
        for n in range(2):
            vpad[n, f, 7:8, :] = corner[f : f + 1, 128 * n : 128 * n + 128]
    for r in range(9):
        for f in range(3):
            for s in range(3):
                block = take(flat, (r * 3 + f) * PITCH + 7 + s, 16, 2).astype(BF16)
                for t in range(3):
                    for p in range(3):
                        if frame_of(t, p) != f:
                            continue
                        for q in range(3):
                            i, odd = divmod(r - q, 2)
                            if odd or not 0 <= i < 4:
                                continue
                            tap = (p * 3 + q) * 3 + s
                            patches[
                                (t * 4 + i) * 16 : (t * 4 + i) * 16 + 16, tap * CI : tap * CI + CI
                            ] = block
    unit = identity(CI)
    for tap in range(TAPS):
        pt[tap * CI : tap * CI + CI, :] = nt(unit, patches[:, tap * CI : tap * CI + CI]).astype(BF16)
    swaps = []
    for n in range(4):
        base = pl.multiple_of(n * 2 * BLOCK + (1 - core) * BLOCK, 32)
        swaps.append(remote(pt.at[pl.ds(base, BLOCK), :], pts.at[n], c_s.at[n], c_r.at[n], sibling))
        swaps[-1].start()

    passed = []
    for at, n in enumerate((1, 3, 2)):
        direct[at].wait_recv()
        ref = kt.at[pl.ds(shard_rows(4 - n), 32), pl.ds(ROUND, DIRECT)]
        passed.append(remote(ref, ref, c_s.at[3 + n], c_r.at[3 + n], sibling))
        passed[-1].start()
    for at, n in enumerate((1, 3, 2)):
        for m in range(3):
            relayed[at * 3 + m].wait_recv()
        ref = kt.at[pl.ds(shard_rows(4 - n), 32), pl.ds(0, ROUND)]
        passed.append(remote(ref, ref, c_s.at[6 + n], c_r.at[6 + n], sibling))
        passed[-1].start()
    for copy in passed:
        copy.wait_recv()

    preact = nt(patches[...], kt[...]) + bias[...]
    sigma = jax.nn.sigmoid(preact)
    act_out[...] = (preact * sigma).astype(BF16).reshape(1, 3, 4, 16, CO)
    load_c.wait()
    slope = cotv[...].reshape(TOK, CO).astype(F32) * sigma * (1.0 + preact * (1.0 - sigma))
    delta = slope.astype(BF16)
    dl[...] = delta
    swap_delta = remote(dl, dls, c_s.at[10], c_r.at[10], sibling)
    swap_delta.start()
    delta_f = delta.astype(F32)
    dlx[...] = swap_halves(delta_f).astype(BF16)
    bias_own = jnp.sum(delta_f, axis=0, keepdims=True)

    swap_delta.wait_recv()
    delta_s = dls[...].astype(F32)
    dlsx[...] = swap_halves(delta_s).astype(BF16)
    bias_chip = bias_own + jnp.sum(delta_s, axis=0, keepdims=True)
    by[y] = jnp.broadcast_to(bias_chip, (8, CO))
    for copy in swaps:
        copy.wait_recv()

    low = lax.broadcasted_iota(jnp.int32, (144, 128), 1) < 64
    phase1 = []
    for part in range(2):
        for step in range(6):
            lo_at = pl.multiple_of(part * 2 * BLOCK + core * BLOCK + step * 144, 16)
            hi_at = pl.multiple_of((part + 2) * 2 * BLOCK + core * BLOCK + step * 144, 16)
            here = slice(step * 144, step * 144 + 144)
            lo = nn(pt[pl.ds(lo_at, 144), :], dl[...]) + nn(pts[part, here, :], dls[...])
            hi = nn(pt[pl.ds(hi_at, 144), :], dlx[...]) + nn(pts[part + 2, here, :], dlsx[...])
            for n in range(4):
                cols = slice(128 * (n // 2), 128 * (n // 2) + 128)
                if n % 2:
                    w[part, n, here, :] = jnp.where(low, hi[:, cols], lo[:, cols]).astype(BF16)
                else:
                    w[part, n, here, :] = jnp.where(low, lo[:, cols], hi[:, cols]).astype(BF16)
        for n in (1, 3, 2):
            if part == 0:
                phase1.append(
                    remote(w.at[0, lax.rem(y + n, 4)], ra.at[n - 1], r1_s.at[n - 1], r1_r.at[n - 1], to_y(n))
                )
            else:
                start = pl.multiple_of(16 * (27 * lax.rem(x + n, 4) // 2), 16)
                phase1.append(
                    remote(
                        w.at[1, :, pl.ds(start, WINDOW), :],
                        rb.at[n - 1],
                        r1_s.at[2 + n],
                        r1_r.at[2 + n],
                        to_x(n),
                    )
                )
            phase1[-1].start()
        if part == 0:
            bias_y = [remote(by.at[y], by.at[y], b_s.at[n - 1], b_r.at[n - 1], to_y(n)) for n in (1, 2, 3)]
            for copy in bias_y:
                copy.start()

    g[...] = jnp.zeros_like(g)
    gflat = g.reshape(2 * PLANE, 128)
    for q in range(3):
        for s in range(3):
            d = [
                nn(dl[...], kt[:, ((p * 3 + q) * 3 + s) * CI : ((p * 3 + q) * 3 + s) * CI + CI])
                for p in range(3)
            ]
            frames = [
                d[0][0:64] + d[0][64:128] + d[0][128:192] + d[1][0:64] + d[1][64:128] + d[2][0:64],
                d[1][128:192] + d[2][64:128],
                d[2][128:192],
            ]
            for f in range(3):
                for i in range(4):
                    at = ((q + 2 * i) * 3 + f) * PITCH + 7 + s
                    sofar = take(gflat, at, 16, 2)
                    put(gflat, at, 16, 2, sofar + frames[f][16 * i : 16 * i + 16])
    gl_send[...] = take(gflat, 3 * PITCH + 7, 24, PITCH)
    for f in range(3):
        for n in range(2):
            gc_send[f : f + 1, 128 * n : 128 * n + 128] = g[n, f, 7:8, :]
    edges = [
        remote(gl_send, gl, h_s.at[3], h_r.at[3], to_tile(0, -1)),
        remote(g.at[:, pl.ds(0, 3), pl.ds(8, 32), :], gu, h_s.at[4], h_r.at[4], to_tile(-1, 0)),
        remote(gc_send, gc, h_s.at[5], h_r.at[5], to_tile(-1, -1)),
    ]
    for copy in edges:
        copy.start()

    for copy in bias_y:
        copy.wait_recv()
    bx[x] = by[0] + by[1] + by[2] + by[3]
    bias_x = [remote(bx.at[x], bx.at[x], b_s.at[2 + n], b_r.at[2 + n], to_x(n)) for n in (1, 2, 3)]
    for copy in bias_x:
        copy.start()

    for copy in phase1[:3]:
        copy.wait_recv()
    sa[...] = (
        w[0, y].astype(F32) + ra[0].astype(F32) + ra[1].astype(F32) + ra[2].astype(F32)
    ).astype(BF16)
    phase2 = []
    for n in (1, 3, 2):
        start = pl.multiple_of(16 * (27 * lax.rem(x + n, 4) // 2), 16)
        phase2.append(
            remote(sa.at[pl.ds(start, WINDOW), :], ra2.at[n - 1], r2_s.at[n - 1], r2_r.at[n - 1], to_x(n))
        )
        phase2[-1].start()
    own = pl.multiple_of(16 * (27 * x // 2), 16)
    for copy in phase1[3:]:
        copy.wait_recv()
    sb[...] = (
        w[1, :, pl.ds(own, WINDOW), :].astype(F32)
        + rb[0].astype(F32)
        + rb[1].astype(F32)
        + rb[2].astype(F32)
    ).astype(BF16)
    for n in (1, 3, 2):
        phase2.append(
            remote(sb.at[lax.rem(y + n, 4)], rb2.at[n - 1], r2_s.at[2 + n], r2_r.at[2 + n], to_y(n))
        )
        phase2[-1].start()

    for copy in edges:
        copy.wait_recv()
    for f in range(3):
        for n in range(2):
            g[n, 24 + f, 8:40, :] += jnp.where(row < 7, gu[n, f], 0.0)
    sofar = take(gflat, 3 * PITCH + 39, 24, PITCH)
    put(gflat, 3 * PITCH + 39, 24, PITCH, sofar + jnp.where(col < 7, gl[...], 0.0))
    corner = jnp.where((row < 7) & (col < 7), gc[...], 0.0)
    for f in range(3):
        for n in range(2):
            g[n, 24 + f, 39:40, :] += corner[f : f + 1, 128 * n : 128 * n + 128]
    for f in range(3):
        for r in range(8):
            for n in range(2):
                vg_out[0, f, r, :, 128 * n : 128 * n + 128] = g[n, (r + 1) * 3 + f, 8:40, :].astype(BF16)

    for copy in bias_x:
        copy.wait_recv()
    bz[z] = bx[0] + bx[1] + bx[2] + bx[3]
    bias_z = [remote(bz.at[z], bz.at[z], b_s.at[5 + n], b_r.at[5 + n], to_z(n)) for n in range(1, 8)]
    for copy in bias_z:
        copy.start()

    odd = lax.rem(y, 2) == 1
    offset = 8 * lax.rem(x, 2)
    first_half = lax.broadcasted_iota(jnp.int32, (64, 128), 1) < 64
    tt[:, WINDOW:, :] = jnp.zeros((2, 24, 128), F32)
    for part in range(2):
        for copy in phase2[3 * part : 3 * part + 3]:
            copy.wait_recv()
        if part == 0:
            total = sa[pl.ds(own, WINDOW), :].astype(F32)
            for n in range(3):
                total = total + ra2[n].astype(F32)
        else:
            total = sb[y].astype(F32)
            for n in range(3):
                total = total + rb2[n].astype(F32)
        tt[part, 0:WINDOW, :] = jnp.where(odd, pltpu.roll(total, 64, 1), total)
        for half in range(2):
            u = tt[part, pl.ds(offset + PIECE * half, 128), :]
            a, b = u[0:64], u[64:128]
            zz[half * 4 + part] = jnp.where(first_half, a, pltpu.roll(b, 64, 1)).astype(BF16)
            zz[half * 4 + 2 + part] = jnp.where(first_half, pltpu.roll(a, 64, 1), b).astype(BF16)
    phase3 = []
    for n in (4, 3, 5, 2, 6, 1, 7):
        phase3.append(
            remote(zz.at[lax.rem(z + n, 8)], rz.at[n - 1], r3_s.at[n - 1], r3_r.at[n - 1], to_z(n))
        )
        phase3[-1].start()

    for copy in bias_z:
        copy.wait_recv()
    total = bz[0]
    for n in range(1, 8):
        total = total + bz[n]
    bg_out[...] = total[0:1] * FACTOR

    for copy in phase3:
        copy.wait_recv()
    total = zz[z].astype(F32)
    for n in range(7):
        total = total + rz[n].astype(F32)
    total = total * FACTOR
    kg_out[0:64, :] = total[:, 0:64]
    kg_out[64:PIECE, :] = pltpu.roll(total, 64, 1)[0 : PIECE - 64, 0:64]

    for copies in (
        first, halos, direct, relayed, swaps, passed, [swap_delta], phase1, bias_y, edges, bias_x,
        phase2, bias_z, phase3,
    ):
        for copy in copies:
            copy.wait_send()


def body(video, kernel, bias_vec, cotangent):
    dma = pltpu.SemaphoreType.DMA
    vmem = pltpu.VMEM
    activated, video_grad, kernel_grad, bias_grad = pl.pallas_call(
        kernel_body,
        out_shape=(
            jax.ShapeDtypeStruct((1, 3, 4, 16, CO), BF16),
            jax.ShapeDtypeStruct((1, 3, 8, 32, CI), BF16),
            jax.ShapeDtypeStruct((PIECE, SHARD), F32),
            jax.ShapeDtypeStruct((1, CO), F32),
        ),
        in_specs=[
            pl.BlockSpec(memory_space=pl.ANY),
            pl.BlockSpec(memory_space=pl.ANY),
            pl.BlockSpec(memory_space=pltpu.VMEM),
            pl.BlockSpec(memory_space=pl.ANY),
        ],
        out_specs=tuple(pl.BlockSpec(memory_space=pltpu.VMEM) for _ in range(4)),
        scratch_shapes=[
            vmem((KROWS, SHARD), BF16),
            vmem((CO, KROWS), BF16),
            vmem((3, 8, 32, CI), BF16),
            vmem((3, 4, 16, CO), BF16),
            vmem((2, 27, PITCH, 128), F32),
            vmem((24, CI), F32),
            vmem((8, CI), F32),
            vmem((24, CI), F32),
            vmem((3, 32, CI), BF16),
            vmem((8, CI), F32),
            vmem((TOK, KROWS), BF16),
            vmem((KROWS, TOK), BF16),
            vmem((4, BLOCK, TOK), BF16),
            vmem((TOK, CO), BF16),
            vmem((TOK, CO), BF16),
            vmem((TOK, CO), BF16),
            vmem((TOK, CO), BF16),
            vmem((2, 4, BLOCK, 128), BF16),
            vmem((3, BLOCK, 128), BF16),
            vmem((3, 4, WINDOW, 128), BF16),
            vmem((BLOCK, 128), BF16),
            vmem((4, WINDOW, 128), BF16),
            vmem((3, WINDOW, 128), BF16),
            vmem((3, WINDOW, 128), BF16),
            vmem((2, WINDOW + 24, 128), F32),
            vmem((8, 64, 128), BF16),
            vmem((7, 64, 128), BF16),
            vmem((4, 8, CO), F32),
            vmem((4, 8, CO), F32),
            vmem((8, 8, CO), F32),
            vmem((2, 27, PITCH, 128), F32),
            vmem((24, CI), F32),
            vmem((8, CI), F32),
            vmem((2, 3, 32, 128), F32),
            vmem((24, CI), F32),
            vmem((8, CI), F32),
            dma((3,)),
            dma((15,)),
            dma((15,)),
            dma((6,)),
            dma((6,)),
            dma((11,)),
            dma((11,)),
            dma((6,)),
            dma((6,)),
            dma((6,)),
            dma((6,)),
            dma((7,)),
            dma((7,)),
            dma((13,)),
            dma((13,)),
        ],
        compiler_params=pltpu.CompilerParams(
            collective_id=0, has_side_effects=True, vmem_limit_bytes=48 * 2**20
        ),
    )(video, kernel, bias_vec.reshape(1, CO), cotangent)
    return activated, video_grad, kernel_grad, bias_grad.reshape(CO)


def solution(mesh):
    return jax.shard_map(
        body,
        mesh=mesh,
        in_specs=(
            P("fsdp", None, "row", "col", None),
            P(None, "fsdp"),
            P(),
            P("fsdp", None, "row", "col", None),
        ),
        out_specs=(
            P("fsdp", None, "row", "col", None),
            P("fsdp", None, "row", "col", None),
            P(("row", "col"), "fsdp"),
            P(),
        ),
        check_vma=False,
    )
```

time: 715 us -> 60.7 us (0.08)
  the two profiles are of different devices: /device:TPU:2 before, /device:TPU:22 now
where the time goes in v1:
time: 60.7 us; the launch traced here: 60.6 us
  Pallas kernels  55.3 us (91%)
  local copies, waits for them, and re-layouts  4.61 us (8%)
  between operations  0.7 us (1%)
    pallas_call x1, Pallas kernels, body(): pl.pallas_call(kernel_body, out_shape=(jax.ShapeDtypeStruct((1, 3, 4, 16,...  55.3 us
    unnamed x11, local copies, waits for them, and re-layouts  4.61 us

profile of v1, /device:TPU:22, one launch (start us, length us, event | category | flops | bytes accessed | tf_op | source)
XLA Modules:
  0.0 60.6 jit_solution(16074300433016444074)
XLA Ops:
  0.6 0.0 copy-start.1
  0.6 0.0 copy-start.2
  0.7 0.0 copy-start
  0.7 1.9 %copy.8.kernel = bf16[6912,64]{1,0:T(8,128)(2,1)S(1)} copy(bf16[6912,64]{0,1:T(8,128)(2,1)} %param.5) | data formatting | bytes 1769472 | tf_op args[1]
  2.6 0.0 copy-done.1
  2.6 0.0 copy-done.2
  2.6 0.0 copy-done
  2.6 55.3 %shard_map.75 = (bf16[1,3,4,16,256]{4,3,2,1,0:T(8,128)(2,1)S(1)}, bf16[1,3,8,32,256]{4,3,2,1,0:T(8,128)(2,1)S(1)}, f32[108,64]{1,0:T(8,128)S(1)}, f32[1,256]{1,0:T(1,128)S(1)}) custom-call(bf16[1,3,8,32,256]{4,3,2,1,0:T(8,128)(2,1)S(1)} %copy-done, bf16[6912,64]{1,0:T(8,128)(2,1)S(1)} %copy.8.kernel, f32[1,256]{1,0:T(1,128)S(1)} %bitcast.2, ...), custom_call_target="tpu_custom_call" | custom-call | tf_op jit(solution)/shard_map/pallas_call | solution.py:480
  57.9 0.7 %copy.9 = f32[108,64]{0,1:T(8,128)} copy(f32[108,64]{1,0:T(8,128)S(1)} %get-tuple-element.14) | data formatting | bytes 55296
  58.6 0.6 %copy.13 = bf16[1,3,4,16,256]{4,3,2,1,0:T(8,128)(2,1)} copy(bf16[1,3,4,16,256]{4,3,2,1,0:T(8,128)(2,1)S(1)} %get-tuple-element.20) | data formatting | bytes 196608
  59.3 0.7 %copy.14 = bf16[1,3,8,32,256]{4,3,2,1,0:T(8,128)(2,1)} copy(bf16[1,3,8,32,256]{4,3,2,1,0:T(8,128)(2,1)S(1)} %get-tuple-element.21) | data formatting | bytes 786432
  60.0 0.6 copy.15
Async XLA Ops:
  0.6 2.0 %copy-start.1 = (bf16[1,3,4,16,256]{4,3,2,1,0:T(8,128)(2,1)S(1)}, bf16[1,3,4,16,256]{4,3,2,1,0:T(8,128)(2,1)}, u32[]{:S(2)}) copy-start(bf16[1,3,4,16,256]{4,3,2,1,0:T(8,128)(2,1)} %cot.1) | copy-start | bytes 294916
  0.6 2.0 %copy-start.2 = (f32[256]{0:T(256)S(1)}, f32[256]{0:T(256)}, u32[]{:S(2)}) copy-start(f32[256]{0:T(256)} %param.6) | copy-start | bytes 3076
  0.7 2.0 %copy-start = (bf16[1,3,8,32,256]{4,3,2,1,0:T(8,128)(2,1)S(1)}, bf16[1,3,8,32,256]{4,3,2,1,0:T(8,128)(2,1)}, u32[]{:S(2)}) copy-start(bf16[1,3,8,32,256]{4,3,2,1,0:T(8,128)(2,1)} %video.1) | copy-start | bytes 1179652
